TPU v7x, 256 devices: a whole 4x4x8 slice. The times are simulated.
256 devices in a mesh: dp: 64 (over z, x, core), tensor: 4 (over y).
Axes of the slice: x: 4, y: 4, z: 8, core: 2. Of those that a mesh axis runs over, the one named last changes fastest.
Arguments:
- acts: bfloat16 [12288, 8192], P('dp', 'tensor'), may hold values from -6 to 6
- out_grads: bfloat16 [12288, 2, 28672], P('dp', None, 'tensor'), may hold values from -16 to 16
- projectors: bfloat16 [2, 8192, 64], replicated, may hold values from -0.75 to 0.75
- moment_first: float32 [28672, 128], P(('tensor', 'dp')), may hold values from -0.12 to 0.12
- moment_second: float32 [28672, 128], P(('tensor', 'dp')), may hold values from 1e-06 to 0.0001
Outputs:
- update: bfloat16 [2, 8192, 28672], P(None, 'dp', 'tensor')
- new_first: float32 [28672, 128], P(('tensor', 'dp'))
- new_second: float32 [28672, 128], P(('tensor', 'dp'))
All inputs are finite; a program needn't handle non-finite values.
Results may differ from a plain program's by a relative error of at most 0.006.
Values may be sent and summed in bfloat16 or wider, within the bound.
A program may use at most 128 MiB of HBM per device.

v0:
```python
import jax
import jax.numpy as jnp
from jax import lax
from jax.sharding import PartitionSpec as P

corr_one = 1.0 - 0.9**10
corr_two = 1.0 - 0.999**10


def local(acts, out_grads, projectors, moment_first, moment_second):
    rank = projectors.shape[2]
    width_part = acts.shape[1]
    tensor_idx = lax.axis_index("tensor")
    proj_rows = lax.dynamic_slice_in_dim(projectors, tensor_idx * width_part, width_part, 1)
    partial_xp = jnp.concatenate(
        [jnp.dot(acts, proj_rows[k], preferred_element_type=jnp.float32) for k in range(2)], axis=1
    )
    reduced = lax.psum(partial_xp, "tensor").astype(jnp.bfloat16)
    dp_count = lax.axis_size("dp")
    total_tokens = acts.shape[0] * dp_count
    reduced_all = lax.all_gather(reduced, "dp", axis=0, tiled=True)
    columns = lax.all_to_all(out_grads, "dp", split_axis=2, concat_axis=0, tiled=True)
    grad = jnp.concatenate(
        [
            lax.dot_general(
                columns[:, k, :],
                reduced_all[:, k * rank : (k + 1) * rank],
                (((0,), (0,)), ((), ())),
                preferred_element_type=jnp.float32,
            )
            for k in range(2)
        ],
        axis=1,
    )
    grad = grad / jnp.float32(total_tokens)
    new_first = 0.9 * moment_first + 0.1 * grad
    new_second = 0.999 * moment_second + 0.001 * grad * grad
    normed = (new_first / corr_one / (jnp.sqrt(new_second / corr_two) + 1e-08)).astype(jnp.bfloat16)
    row_count = projectors.shape[1] // dp_count
    dp_idx = lax.axis_index("dp")
    decode_rows = lax.dynamic_slice_in_dim(projectors, dp_idx * row_count, row_count, 1)
    piece = lax.all_gather(normed, "dp", axis=0, tiled=True)
    update = jnp.stack(
        [
            lax.dot_general(
                decode_rows[k],
                piece[:, k * rank : (k + 1) * rank],
                (((1,), (1,)), ((), ())),
                preferred_element_type=jnp.float32,
            ).astype(jnp.bfloat16)
            for k in range(2)
        ],
        axis=0,
    )
    return (update, new_first, new_second)


def solution(mesh):
    return jax.shard_map(
        local,
        mesh=mesh,
        in_specs=(
            P("dp", "tensor"),
            P("dp", None, "tensor"),
            P(),
            P(("tensor", "dp"), None),
            P(("tensor", "dp"), None),
        ),
        out_specs=(P(None, "dp", "tensor"), P(("tensor", "dp"), None), P(("tensor", "dp"), None)),
        check_vma=False,
    )
```

profile of v0, /device:TPU:1, one launch (start us, length us, event | category | flops | bytes accessed | tf_op | source)
XLA Modules:
  0.0 331.5 jit_solution(17090508039647898169)
XLA Ops:
  7.2 24.8 %copy.42 = bf16[192,2,7168]{0,1,2:T(2,128)(2,1)} copy(bf16[192,2,7168]{2,1,0:T(2,128)(2,1)} %param.6) | data formatting | bytes 11010048 | tf_op args[1]
  32.0 13.3 %all-to-all-start = ((bf16[192,2,7168]{0,1,2:T(2,128)(2,1)}), bf16[192,2,7168]{0,1,2:T(2,128)(2,1)}, u32[]{:S(2)}, u32[]{:S(2)}) async-start(bf16[192,2,7168]{0,1,2:T(2,128)(2,1)} %copy.42), calls=%async_computation | async-start | bytes 14680064 | tf_op jit(solution)/shard_map/all_to_all | solution.py:22
  45.3 0.0 all-gather.3.cloned.1.call-start
  45.3 0.4 convolution_bitcast_fusion.1
  45.7 0.4 convolution_bitcast_fusion
  46.1 0.1 pad_maximum_fusion.1
  46.2 16.5 %psum.7 = bf16[192,128]{1,0:T(8,128)(2,1)} all-reduce(f32[192,128]{1,0:T(8,128)S(1)} %pad_maximum_fusion.1), channel_id=1, replica_groups=mesh['dp'=64,'tensor'=4] {'tensor'}, use_global_device_ids=true, to_apply=%region_0.0 | all-reduce | flops 24576 | bytes 147456 | tf_op jit(solution)/shard_map/psum | solution.py:18
  62.7 0.0 all-gather.3.cloned.1.call-update
  62.7 0.0 all-gather.5.cloned.1.call-start
  62.8 0.1 copy.39
  62.9 0.1 copy.46
  63.0 152.0 %all-to-all-done = bf16[192,2,7168]{0,1,2:T(2,128)(2,1)} async-done(((bf16[192,2,7168]{0,1,2:T(2,128)(2,1)}), bf16[192,2,7168]{0,1,2:T(2,128)(2,1)}, u32[]{:S(2)}, u32[]{:S(2)}) %all-to-all-start) | async-done | bytes 5505056 | tf_op jit(solution)/shard_map/all_to_all | solution.py:22
  215.0 18.1 %copy.43 = bf16[192,2,64,112]{3,0,2,1:T(8,128)(2,1)} copy(bf16[192,2,64,112]{0,1,3,2:T(2,128)(2,1)} %bitcast.5) | data formatting | bytes 11010048 | tf_op jit(solution)/shard_map/all_to_all | solution.py:22
  233.1 4.8 %fusion.11 = f32[112,64]{0,1:T(8,128)S(1)} fusion(bf16[12288,2,112]{2,0,1:T(8,128)(2,1)} %bitcast.42, bf16[12288,128]{1,0:T(8,128)(2,1)} %all-gather.3.cloned.1.call-done), kind=kOutput, calls=%fused_computation.16 | convolution fusion | flops 176160768 | bytes 6320128 | tf_op jit(solution)/shard_map/dot_general | solution.py:25
  237.9 2.9 fusion.8
  240.9 0.1 divide_convert_fusion
  240.9 0.7 copy.47
  241.6 0.0 all-gather.5.cloned.1.call-update
  241.7 0.7 copy.48
  242.4 0.7 copy.49
  243.1 76.0 %all-gather.5.cloned.1.call-done = bf16[7168,128]{1,0:T(8,128)(2,1)} async-done(((bf16[112,128]{1,0:T(8,128)(2,1)}), bf16[7168,128]{1,0:T(8,128)(2,1)}) %all-gather.5.cloned.1.call-update) | async-done | bytes 1835024 | tf_op jit(solution)/shard_map/all_gather | solution.py:42
  319.2 2.6 fusion.1
  321.8 0.7 fusion
  322.5 2.2 pad_maximum_fusion
  (13 shorter events, 0.0 us)
Async XLA Ops:
  7.2 38.2 %copy-start = (bf16[2,8192,64]{1,2,0:T(8,128)(2,1)S(1)}, bf16[2,8192,64]{1,2,0:T(8,128)(2,1)}, u32[]{:S(2)}) copy-start(bf16[2,8192,64]{1,2,0:T(8,128)(2,1)} %param.7) | copy-start | bytes 6291460
  32.0 13.4 %copy-start.3 = (bf16[192,2048]{1,0:T(8,128)(2,1)S(1)}, bf16[192,2048]{1,0:T(8,128)(2,1)}, u32[]{:S(2)}) copy-start(bf16[192,2048]{1,0:T(8,128)(2,1)} %param.5) | copy-start | bytes 2359300
  32.0 30.8 %copy-start.4 = (f32[112,128]{1,0:T(8,128)S(1)}, f32[112,128]{1,0:T(8,128)}, u32[]{:S(2)}) copy-start(f32[112,128]{1,0:T(8,128)} %param.8) | copy-start | bytes 172036
  32.0 30.9 %copy-start.5 = (f32[112,128]{1,0:T(8,128)S(1)}, f32[112,128]{1,0:T(8,128)}, u32[]{:S(2)}) copy-start(f32[112,128]{1,0:T(8,128)} %param.9) | copy-start | bytes 172036
  32.0 183.1 %all-to-all-start = ((bf16[192,2,7168]{0,1,2:T(2,128)(2,1)}), bf16[192,2,7168]{0,1,2:T(2,128)(2,1)}, u32[]{:S(2)}, u32[]{:S(2)}) async-start(bf16[192,2,7168]{0,1,2:T(2,128)(2,1)} %copy.42), calls=%async_computation | async-start | bytes 14680064 | tf_op jit(solution)/shard_map/all_to_all | solution.py:22
  45.3 187.8 %all-gather.3.cloned.1.call-start = ((), (), s32[]{:S(2)}) async-start(), calls=%async_computation.1 | async-start | bytes 3194880 | tf_op jit(solution)/shard_map/all_gather | solution.py:21
  62.7 256.4 %all-gather.5.cloned.1.call-start = ((), (), s32[]{:S(2)}) async-start(), calls=%async_computation.2 | async-start | bytes 1863680 | tf_op jit(solution)/shard_map/all_gather | solution.py:42
  233.1 4.8 %copy-start.2 = (bf16[192,2,64,112]{3,0,2,1:T(8,128)(2,1)S(1)}, bf16[192,2,64,112]{3,0,2,1:T(8,128)(2,1)}, u32[]{:S(2)}) copy-start(bf16[192,2,64,112]{3,0,2,1:T(8,128)(2,1)} %copy.43) | copy-start | bytes 16515076
  319.2 2.6 copy-start.1
Sparse Core Ops, SparseCore 0:
  62.9 104.7 all-gather.2
  241.8 77.3 all-gather.4
where the time goes:
time: 333 us; the launch traced here: 331 us
  waiting for transfers between devices  228 us (68%)
  local copies, waits for them, and re-layouts  45.2 us (14%)
  blocking collectives  16.5 us (5%)
  between operations  14.2 us (4%)
  starting transfers between devices  13.4 us (4%)
  matrix products  11.7 us (4%)
    all_to_all x1, waiting for transfers between devices, local(): lax.all_to_all(out_grads, 'dp', split_axis=2, concat_axis=0, tiled=True)  152 us
    all_gather x1, waiting for transfers between devices, local(): piece = lax.all_gather(normed, 'dp', axis=0, tiled=True)  76 us
    unnamed x17, local copies, waits for them, and re-layouts  26.4 us
    all_to_all x1, local copies, waits for them, and re-layouts, local(): lax.all_to_all(out_grads, 'dp', split_axis=2, concat_axis=0, tiled=True)  18.1 us
    psum x1, blocking collectives, local(): reduced = lax.psum(partial_xp, 'tensor').astype(jnp.bfloat16)  16.5 us
    all_to_all x1, starting transfers between devices, local(): lax.all_to_all(out_grads, 'dp', split_axis=2, concat_axis=0, tiled=True)  13.3 us
    dot_general x2, matrix products, local(): lax.dot_general(columns[:, k, :], reduced_all[:, k * rank:(k + 1) * rank]...  7.72 us
  transfers between devices with their start and end apart: 3, of which 2 were waited for; matrix products, arithmetic and copies ran while one was open for 6% of the time, Pallas kernels for 0%

commit v1 on v0

v1 whole, which is shorter than its diff:
```python
import functools

import jax
import jax.numpy as jnp
from jax import lax
from jax.experimental import pallas as pl
from jax.experimental.pallas import tpu as pltpu
from jax.sharding import PartitionSpec as P

MESH = pl.DeviceIdType.MESH
corr_one = 1.0 - 0.9**10
corr_two = 1.0 - 0.999**10

NZ, NX, NC, NY = 8, 4, 2, 4
bf16, f32 = jnp.bfloat16, jnp.float32


def adam(grad, first, second):
    new_first = 0.9 * first + 0.1 * grad
    new_second = 0.999 * second + 0.001 * grad * grad
    return new_first, new_second


def normalize(new_first, new_second):
    return new_first / corr_one / (jnp.sqrt(new_second / corr_two) + 1e-08)


def reduce_gather(
    tokens, acts, proj, grads, first, second,
    gathered, grad_out,
    acts_v, proj_v, grads_v, first_v, second_v,
    xp_own, xp_in, part, part_send, core_in, x_send, x_in, z_send, z_own, z_in,
    in_sem, og_sem, y_s, y_r, c_s, c_r, x_s, x_r, z_s, z_r,
    gz_s, gz_r, gx_s, gx_r, gc_s, gc_r,
):
    t_count, _, columns = grads.shape
    group = columns // NZ
    own = group // (NX * NC)
    width = acts.shape[1]
    rank = proj.shape[1]
    pair = 2 * rank
    dp, y = lax.axis_index("dp"), lax.axis_index("tensor")
    z, x, c = dp // (NX * NC), lax.rem(dp // NC, NX), lax.rem(dp, NC)

    def zdev(j):
        return ((lax.rem(z + j, NZ) * NX + x) * NC + c, y)

    def xdev(j):
        return ((z * NX + lax.rem(x + j, NX)) * NC + c, y)

    def ydev(j):
        return (dp, lax.rem(y + j, NY))

    sibling = ((z * NX + x) * NC + (1 - c), y)

    def remote(src, dst, s, r, device):
        return pltpu.make_async_remote_copy(
            src_ref=src, dst_ref=dst, send_sem=s, recv_sem=r, device_id=device, device_id_type=MESH
        )

    load_acts = pltpu.make_async_copy(acts, acts_v, in_sem.at[0])
    load_proj = pltpu.make_async_copy(proj.at[:, :, pl.ds(pl.multiple_of(y * width, 128), width)], proj_v, in_sem.at[1])
    load_first = pltpu.make_async_copy(first, first_v, in_sem.at[2])
    load_second = pltpu.make_async_copy(second, second_v, in_sem.at[3])
    load_acts.start()
    load_proj.start()

    def offset(s):
        return NZ // 2 + (1 - 2 * lax.rem(s, 2)) * ((s + 1) // 2)

    def load_group(s):
        g = lax.rem(z + offset(s), NZ)
        span = pl.ds(pl.multiple_of(g * group, 128), group)
        return pltpu.make_async_copy(grads.at[:, :, span], grads_v.at[s], og_sem.at[s])

    @pl.loop(0, NZ)
    def _(s):
        load_group(s).start()

    load_first.start()
    load_second.start()

    barrier = pltpu.get_barrier_semaphore()
    peers = [zdev(j) for j in range(1, NZ)] + [xdev(j) for j in range(1, NX)] + [ydev(j) for j in range(1, NY)] + [sibling]
    for peer in peers:
        pl.semaphore_signal(barrier, inc=1, device_id=peer, device_id_type=MESH)

    load_acts.wait()
    load_proj.wait()
    nt = (((1,), (1,)), ((), ()))
    xp_own[...] = lax.dot_general(acts_v[...], proj_v[...].reshape(pair, width), nt, preferred_element_type=f32)
    pl.semaphore_wait(barrier, len(peers))

    y_copies = [remote(xp_own, xp_in.at[j - 1], y_s.at[j - 1], y_r.at[j - 1], ydev(j)) for j in range(1, NY)]
    for copy in y_copies:
        copy.start()
    row = lax.broadcasted_iota(jnp.int32, (2 * t_count, t_count), 0)
    col = lax.broadcasted_iota(jnp.int32, (2 * t_count, t_count), 1)
    spread = jnp.where(row // 2 == col, 1.0, 0.0).astype(bf16)
    for copy in y_copies:
        copy.wait_recv()
    reduced = (xp_own[...] + xp_in[0] + xp_in[1] + xp_in[2]).astype(bf16)
    weights = lax.dot_general(reduced, spread, (((0,), (1,)), ((), ())), preferred_element_type=f32)
    row = lax.broadcasted_iota(jnp.int32, (pair, 2 * t_count), 0)
    col = lax.broadcasted_iota(jnp.int32, (pair, 2 * t_count), 1)
    weights = jnp.where(lax.rem(col, 2) == row // rank, weights, 0.0).astype(bf16)

    def core_copy(s):
        return remote(part_send.at[s, :, 1 - c], core_in.at[s], c_s.at[s], c_r.at[s], sibling)

    def x_copy(s, j):
        return remote(x_send.at[s, lax.rem(x + j, NX)], x_in.at[s, j - 1], x_s.at[s, j - 1], x_r.at[s, j - 1], xdev(j))

    def z_copy(s):
        j = offset(s)
        return remote(z_send.at[s], z_in.at[s], z_s.at[s], z_r.at[s], zdev(j))

    lag = 2

    @pl.loop(0, NZ + lag)
    def _(step):
        @pl.when(step < NZ)
        def _():
            load_group(step).wait()
            block = grads_v[step].reshape(2 * t_count, group)
            terms = jnp.dot(weights, block, preferred_element_type=f32).T.reshape(NX, NC, own, pair)
            part[step] = terms
            part_send[step] = terms.astype(bf16)
            core_copy(step).start()

        @pl.when(step >= lag)
        def _():
            s = step - lag
            core_copy(s).wait_recv()
            x_send[s] = (part[s, :, c] + core_in[s].astype(f32)).astype(bf16)
            for j in (2, 1, 3):
                x_copy(s, j).start()

    def x_sum(s):
        for j in range(1, NX):
            x_copy(s, j).wait_recv()
        total = part[s, x, c] + core_in[s, x].astype(f32)
        for j in range(NX - 1):
            total += x_in[s, j].astype(f32)
        return total

    @pl.loop(0, NZ - 1)
    def _(s):
        z_send[s] = x_sum(s).astype(bf16)
        z_copy(s).start()

    total = x_sum(NZ - 1)
    for s in range(NZ - 1):
        z_copy(s).wait_recv()
        total += z_in[s].astype(f32)
    grad = total / f32(tokens)
    grad_out[...] = grad
    load_first.wait()
    load_second.wait()
    gathered[z, x, c] = normalize(*adam(grad, first_v[...], second_v[...])).astype(bf16)

    def gz_copy(j):
        here = gathered.at[z, x, c]
        return remote(here, here, gz_s.at[j - 1], gz_r.at[j - 1], zdev(j))

    def gz_arrival(j):
        here = gathered.at[lax.rem(z + NZ - j, NZ), x, c]
        return remote(here, here, gz_s.at[j - 1], gz_r.at[j - 1], zdev(j))

    def near(s):
        return offset(NZ - 1 - s)

    def gx_copy(s, j):
        here = gathered.at[lax.rem(z + NZ - near(s), NZ), x, c]
        return remote(here, here, gx_s.at[s, j - 1], gx_r.at[s, j - 1], xdev(j))

    def gx_arrival(s, j):
        here = gathered.at[lax.rem(z + NZ - near(s), NZ), lax.rem(x + NX - j, NX), c]
        return remote(here, here, gx_s.at[s, j - 1], gx_r.at[s, j - 1], xdev(j))

    def gc_copy(s, j):
        here = gathered.at[lax.rem(z + NZ - near(s), NZ), lax.rem(x + NX - j, NX), c]
        return remote(here, here, gc_s.at[s, j], gc_r.at[s, j], sibling)

    def gc_arrival(s, j):
        here = gathered.at[lax.rem(z + NZ - near(s), NZ), lax.rem(x + NX - j, NX), 1 - c]
        return remote(here, here, gc_s.at[s, j], gc_r.at[s, j], sibling)

    for j in (4, 3, 5, 2, 6, 1, 7):
        gz_copy(j).start()

    @pl.loop(0, NZ)
    def _(s):
        @pl.when(s > 0)
        def _():
            gz_arrival(near(s)).wait_recv()

        for j in (2, 1, 3):
            gx_copy(s, j).start()
        gc_copy(s, 0).start()

    @pl.loop(0, NZ)
    def _(s):
        for j in (1, 3, 2):
            gx_arrival(s, j).wait_recv()
            gc_copy(s, j).start()

    for copy in y_copies:
        copy.wait_send()
    for j in range(1, NZ):
        gz_copy(j).wait_send()

    @pl.loop(0, NZ)
    def _(s):
        core_copy(s).wait_send()
        for j in range(1, NX):
            x_copy(s, j).wait_send()

        @pl.when(s < NZ - 1)
        def _():
            z_copy(s).wait_send()

        for j in range(1, NX):
            gx_copy(s, j).wait_send()
        for j in range(NX):
            gc_copy(s, j).wait_send()
            gc_arrival(s, j).wait_recv()


def decode(normed, grad, first, second, proj, update, new_first, new_second, proj_v, out_v, in_sem, out_sem):
    columns = normed.shape[0]
    rank, rows = proj_v.shape[1], proj_v.shape[2]
    dp = lax.axis_index("dp")
    load = pltpu.make_async_copy(proj.at[:, :, pl.ds(pl.multiple_of(dp * rows, 128), rows)], proj_v, in_sem)
    load.start()
    new_first[...], new_second[...] = adam(grad[...], first[...], second[...])
    load.wait()
    flat = proj_v[...].reshape(2 * rank, rows)
    flat = jnp.concatenate([flat, flat], axis=1)
    row = lax.broadcasted_iota(jnp.int32, flat.shape, 0)
    col = lax.broadcasted_iota(jnp.int32, flat.shape, 1)
    flat = jnp.where(row // rank == col // rows, flat.astype(f32), 0.0).T.astype(bf16)
    chunk = columns // NZ

    def store(s):
        return pltpu.make_async_copy(out_v.at[s], update.at[:, :, pl.ds(pl.multiple_of(s * chunk, 128), chunk)], out_sem.at[s])

    @pl.loop(0, NZ)
    def _(s):
        block = normed[pl.ds(pl.multiple_of(s * chunk, 16), chunk), :]
        out = lax.dot_general(flat, block, (((1,), (1,)), ((), ())), preferred_element_type=f32)
        out_v[s] = out.astype(bf16).reshape(2, rows, chunk)
        store(s).start()

    @pl.loop(0, NZ)
    def _(s):
        store(s).wait()


def local(acts, out_grads, projectors, moment_first, moment_second):
    t_count, width = acts.shape
    columns = out_grads.shape[2]
    rank = projectors.shape[2]
    pair = 2 * rank
    dp_count = lax.axis_size("dp")
    own = columns // dp_count
    group = columns // NZ
    proj = jnp.swapaxes(projectors, 1, 2)
    hbm = pl.BlockSpec(memory_space=pl.ANY)
    vmem = pl.BlockSpec(memory_space=pltpu.VMEM)
    dma = pltpu.SemaphoreType.DMA
    gathered, grad = pl.pallas_call(
        functools.partial(reduce_gather, t_count * dp_count),
        out_shape=(
            jax.ShapeDtypeStruct((NZ, NX, NC, own, pair), bf16),
            jax.ShapeDtypeStruct((own, pair), f32),
        ),
        in_specs=[hbm] * 5,
        out_specs=(vmem, vmem),
        scratch_shapes=[
            pltpu.VMEM((t_count, width), bf16),
            pltpu.VMEM((2, rank, width), bf16),
            pltpu.VMEM((NZ, t_count, 2, group), bf16),
            pltpu.VMEM((own, pair), f32),
            pltpu.VMEM((own, pair), f32),
            pltpu.VMEM((t_count, pair), f32),
            pltpu.VMEM((NY - 1, t_count, pair), f32),
            pltpu.VMEM((NZ, NX, NC, own, pair), f32),
            pltpu.VMEM((NZ, NX, NC, own, pair), bf16),
            pltpu.VMEM((NZ, NX, own, pair), bf16),
            pltpu.VMEM((NZ, NX, own, pair), bf16),
            pltpu.VMEM((NZ, NX - 1, own, pair), bf16),
            pltpu.VMEM((NZ - 1, own, pair), bf16),
            pltpu.VMEM((own, pair), f32),
            pltpu.VMEM((NZ - 1, own, pair), bf16),
            dma((4,)),
            dma((NZ,)),
            dma((NY - 1,)),
            dma((NY - 1,)),
            dma((NZ,)),
            dma((NZ,)),
            dma((NZ, NX - 1)),
            dma((NZ, NX - 1)),
            dma((NZ - 1,)),
            dma((NZ - 1,)),
            dma((NZ - 1,)),
            dma((NZ - 1,)),
            dma((NZ, NX - 1)),
            dma((NZ, NX - 1)),
            dma((NZ, NX)),
            dma((NZ, NX)),
        ],
        compiler_params=pltpu.CompilerParams(collective_id=0, has_side_effects=True, vmem_limit_bytes=40 << 20),
        name="reduce_gather",
    )(acts, proj, out_grads, moment_first, moment_second)
    rows = projectors.shape[1] // dp_count
    return pl.pallas_call(
        decode,
        out_shape=(
            jax.ShapeDtypeStruct((2, rows, columns), bf16),
            jax.ShapeDtypeStruct(moment_first.shape, f32),
            jax.ShapeDtypeStruct(moment_second.shape, f32),
        ),
        in_specs=[vmem] * 4 + [hbm],
        out_specs=(hbm, vmem, vmem),
        scratch_shapes=[
            pltpu.VMEM((2, rank, rows), bf16),
            pltpu.VMEM((NZ, 2, rows, group), bf16),
            dma,
            dma((NZ,)),
        ],
        compiler_params=pltpu.CompilerParams(vmem_limit_bytes=40 << 20),
        name="decode",
    )(gathered.reshape(columns, pair), grad, moment_first, moment_second, proj)


def solution(mesh):
    return jax.shard_map(
        local,
        mesh=mesh,
        in_specs=(
            P("dp", "tensor"),
            P("dp", None, "tensor"),
            P(),
            P(("tensor", "dp"), None),
            P(("tensor", "dp"), None),
        ),
        out_specs=(P(None, "dp", "tensor"), P(("tensor", "dp"), None), P(("tensor", "dp"), None)),
        check_vma=False,
    )
```

time: 333 us -> 65.1 us (0.20)
  waiting for transfers between devices: 228 us -> 0 us
  Pallas kernels: 0 us -> 57.2 us
  local copies, waits for them, and re-layouts: 45.2 us -> 6.92 us
  blocking collectives: 16.5 us -> 0 us
  between operations: 14.2 us -> 0.66 us
  starting transfers between devices: 13.4 us -> 0 us
  matrix products: 11.7 us -> 0 us
    all_to_all x1 -> x0, waiting for transfers between devices: 152 us -> none  [local(): lax.all_to_all(out_grads, 'dp', split_axis=2, concat_axis=0, tiled=True)]
    all_gather x2 -> x0, waiting for transfers between devices: 76.1 us -> none  [the longest x1 76 us: local(): piece = lax.all_gather(normed, 'dp', axis=0, tiled=True)]
    pallas_call x0 -> x2, Pallas kernels: none -> 57.2 us  [the longest x1 53.2 us: local(): pl.pallas_call(functools.partial(reduce_gather, t_count * dp_count), out_...]
    unnamed x17 -> x12, local copies, waits for them, and re-layouts: 26.4 us -> 6.92 us
    all_to_all x1 -> x0, local copies, waits for them, and re-layouts: 18.1 us -> none  [local(): lax.all_to_all(out_grads, 'dp', split_axis=2, concat_axis=0, tiled=True)]
    psum x1 -> x0, blocking collectives: 16.5 us -> none  [local(): reduced = lax.psum(partial_xp, 'tensor').astype(jnp.bfloat16)]
    all_to_all x1 -> x0, starting transfers between devices: 13.3 us -> none  [local(): lax.all_to_all(out_grads, 'dp', split_axis=2, concat_axis=0, tiled=True)]
    dot_general x6 -> x0, matrix products: 11.7 us -> none  [the longest x2 7.72 us: local(): lax.dot_general(columns[:, k, :], reduced_all[:, k * rank:(k + 1) * rank]...]
  transfers between devices with their start and end apart: 3 -> 0, of which waited for: 2 -> 0; matrix products, arithmetic and copies ran while one was open for 6% -> 0% of each run, Pallas kernels for 0% -> 0%
where the time goes in v1:
time: 65.1 us; the launch traced here: 64.8 us
  Pallas kernels  57.2 us (88%)
  local copies, waits for them, and re-layouts  6.92 us (11%)
  between operations  0.66 us (1%)
    pallas_call x1, Pallas kernels, local(): pl.pallas_call(functools.partial(reduce_gather, t_count * dp_count), out_...  53.2 us
    unnamed x12, local copies, waits for them, and re-layouts  6.92 us
    pallas_call x1, Pallas kernels, local(): pl.pallas_call(decode, out_shape=(jax.ShapeDtypeStruct((2, rows, columns)...  4.02 us

profile of v1, /device:TPU:1, one launch (start us, length us, event | category | flops | bytes accessed | tf_op | source)
XLA Modules:
  0.0 64.8 jit_solution(17280481840123385150)
XLA Ops:
  0.6 0.0 copy-start
  0.6 1.6 %copy-done = bf16[2,8192,64]{1,2,0:T(8,128)(2,1)S(1)} copy-done((bf16[2,8192,64]{1,2,0:T(8,128)(2,1)S(1)}, bf16[2,8192,64]{1,2,0:T(8,128)(2,1)}, u32[]{:S(2)}) %copy-start) | copy-done | bytes 2097176
  2.2 0.0 copy-start.2
  2.2 2.6 %copy-done.2 = bf16[192,2,7168]{2,1,0:T(2,128)(2,1)S(1)} copy-done((bf16[192,2,7168]{2,1,0:T(2,128)(2,1)S(1)}, bf16[192,2,7168]{2,1,0:T(2,128)(2,1)}, u32[]{:S(2)}) %copy-start.2) | copy-done | bytes 5505048
  4.8 0.0 copy-start.3
  4.8 1.1 %copy-done.3 = bf16[192,2048]{1,0:T(8,128)(2,1)S(1)} copy-done((bf16[192,2048]{1,0:T(8,128)(2,1)S(1)}, bf16[192,2048]{1,0:T(8,128)(2,1)}, u32[]{:S(2)}) %copy-start.3) | copy-done | bytes 786456
  5.9 0.0 copy-start.4
  5.9 0.8 %copy-done.4 = f32[112,128]{1,0:T(8,128)S(1)} copy-done((f32[112,128]{1,0:T(8,128)S(1)}, f32[112,128]{1,0:T(8,128)}, u32[]{:S(2)}) %copy-start.4) | copy-done | bytes 57368
  6.7 0.0 copy-start.5
  6.7 0.8 %copy-done.5 = f32[112,128]{1,0:T(8,128)S(1)} copy-done((f32[112,128]{1,0:T(8,128)S(1)}, f32[112,128]{1,0:T(8,128)}, u32[]{:S(2)}) %copy-start.5) | copy-done | bytes 57368
  7.6 0.0 copy-start.1
  7.6 53.2 %reduce_gather.1 = (bf16[8,4,2,112,128]{4,3,2,1,0:T(8,128)(2,1)S(1)}, f32[112,128]{1,0:T(8,128)S(1)}) custom-call(bf16[192,2048]{1,0:T(8,128)(2,1)S(1)} %copy-done.3, bf16[2,64,8192]{2,1,0:T(8,128)(2,1)S(1)} %bitcast.2, bf16[192,2,7168]{2,1,0:T(2,128)(2,1)S(1)} %copy-done.2, f32[112,128]{1,0:T(8,128)S(1)} %copy-done.4, f32[112,128]{1,0:T(8,128)S(1)} %copy-done.5), custom_call_target="tpu_custom_call" | custom-call | tf_op jit(solution)/shard_map/reduce_gather/pallas_call | solution.py:272
  60.8 0.0 copy-done.1
  60.8 4.0 %decode.1 = (bf16[2,128,7168]{2,1,0:T(8,128)(2,1)}, f32[112,128]{1,0:T(8,128)}, f32[112,128]{1,0:T(8,128)}) custom-call(bf16[7168,128]{1,0:T(8,128)(2,1)S(1)} %bitcast.4, f32[112,128]{1,0:T(8,128)S(1)} %get-tuple-element.6.grad, f32[112,128]{1,0:T(8,128)S(1)} %copy-done.4, f32[112,128]{1,0:T(8,128)S(1)} %copy-done.5, bf16[2,64,8192]{2,1,0:T(8,128)(2,1)S(1)} %bitcast.3), custom_call_target="tpu_custom_call" | custom-call | tf_op jit(solution)/shard_map/decode/pallas_call | solution.py:317
Async XLA Ops:
  0.6 1.6 %copy-start = (bf16[2,8192,64]{1,2,0:T(8,128)(2,1)S(1)}, bf16[2,8192,64]{1,2,0:T(8,128)(2,1)}, u32[]{:S(2)}) copy-start(bf16[2,8192,64]{1,2,0:T(8,128)(2,1)} %param.7) | copy-start | bytes 6291460
  2.2 2.6 %copy-start.2 = (bf16[192,2,7168]{2,1,0:T(2,128)(2,1)S(1)}, bf16[192,2,7168]{2,1,0:T(2,128)(2,1)}, u32[]{:S(2)}) copy-start(bf16[192,2,7168]{2,1,0:T(2,128)(2,1)} %grads.1) | copy-start | bytes 16515076
  4.8 1.1 %copy-start.3 = (bf16[192,2048]{1,0:T(8,128)(2,1)S(1)}, bf16[192,2048]{1,0:T(8,128)(2,1)}, u32[]{:S(2)}) copy-start(bf16[192,2048]{1,0:T(8,128)(2,1)} %acts.1) | copy-start | bytes 2359300
  5.9 0.8 %copy-start.4 = (f32[112,128]{1,0:T(8,128)S(1)}, f32[112,128]{1,0:T(8,128)}, u32[]{:S(2)}) copy-start(f32[112,128]{1,0:T(8,128)} %first.3) | copy-start | bytes 172036
  6.7 0.8 %copy-start.5 = (f32[112,128]{1,0:T(8,128)S(1)}, f32[112,128]{1,0:T(8,128)}, u32[]{:S(2)}) copy-start(f32[112,128]{1,0:T(8,128)} %second.3) | copy-start | bytes 172036
  7.6 53.2 %copy-start.1 = (bf16[2,8192,64]{1,2,0:T(8,128)(2,1)S(1)}, bf16[2,8192,64]{1,2,0:T(8,128)(2,1)}, u32[]{:S(2)}) copy-start(bf16[2,8192,64]{1,2,0:T(8,128)(2,1)} %param.7) | copy-start | bytes 6291460

commit v2 on v1

v2 whole, which is shorter than its diff:
```python
import functools

import jax
import jax.numpy as jnp
from jax import lax
from jax.experimental import pallas as pl
from jax.experimental.pallas import tpu as pltpu
from jax.sharding import PartitionSpec as P

MESH = pl.DeviceIdType.MESH
corr_one = 1.0 - 0.9**10
corr_two = 1.0 - 0.999**10

NZ, NX, NC, NY = 8, 4, 2, 4
bf16, f32 = jnp.bfloat16, jnp.float32


def adam(grad, first, second):
    new_first = 0.9 * first + 0.1 * grad
    new_second = 0.999 * second + 0.001 * grad * grad
    return new_first, new_second


def normalize(new_first, new_second):
    return new_first / corr_one / (jnp.sqrt(new_second / corr_two) + 1e-08)


def reduce_gather(
    tokens, acts, proj, grads, first, second,
    update, new_first, new_second,
    acts_v, proj_v, rows_v, grads_v, first_v, second_v,
    xp_own, xp_in, part, part_send, core_in, x_send, x_in, z_send, z_in, gathered,
    in_sem, og_sem, y_s, y_r, c_s, c_r, x_s, x_r, z_s, z_r,
    gz_s, gz_r, gx_s, gx_r, gc_s, gc_r,
):
    t_count, _, columns = grads.shape
    group = columns // NZ
    own = group // (NX * NC)
    width = acts.shape[1]
    rank = proj.shape[1]
    pair = 2 * rank
    dp, y = lax.axis_index("dp"), lax.axis_index("tensor")
    z, x, c = dp // (NX * NC), lax.rem(dp // NC, NX), lax.rem(dp, NC)

    def zdev(j):
        return ((lax.rem(z + j, NZ) * NX + x) * NC + c, y)

    def xdev(j):
        return ((z * NX + lax.rem(x + j, NX)) * NC + c, y)

    def ydev(j):
        return (dp, lax.rem(y + j, NY))

    sibling = ((z * NX + x) * NC + (1 - c), y)

    def remote(src, dst, s, r, device):
        return pltpu.make_async_remote_copy(
            src_ref=src, dst_ref=dst, send_sem=s, recv_sem=r, device_id=device, device_id_type=MESH
        )

    load_acts = pltpu.make_async_copy(acts, acts_v, in_sem.at[0])
    load_proj = pltpu.make_async_copy(proj.at[:, :, pl.ds(pl.multiple_of(y * width, 128), width)], proj_v, in_sem.at[1])
    load_first = pltpu.make_async_copy(first, first_v, in_sem.at[2])
    load_second = pltpu.make_async_copy(second, second_v, in_sem.at[3])
    rows = update.shape[1]
    load_rows = pltpu.make_async_copy(proj.at[:, :, pl.ds(pl.multiple_of(dp * rows, 128), rows)], rows_v, in_sem.at[4])
    load_acts.start()
    load_proj.start()
    load_rows.start()

    def offset(s):
        return NZ // 2 + (1 - 2 * lax.rem(s, 2)) * ((s + 1) // 2)

    def load_group(s):
        g = lax.rem(z + offset(s), NZ)
        span = pl.ds(pl.multiple_of(g * group, 128), group)
        return pltpu.make_async_copy(grads.at[:, :, span], grads_v.at[s], og_sem.at[s])

    barrier = pltpu.get_barrier_semaphore()
    peers = [zdev(j) for j in range(1, NZ)] + [xdev(j) for j in range(1, NX)] + [ydev(j) for j in range(1, NY)] + [sibling]
    for peer in peers:
        pl.semaphore_signal(barrier, inc=1, device_id=peer, device_id_type=MESH)

    load_acts.wait()
    load_proj.wait()

    @pl.loop(0, NZ)
    def _(s):
        load_group(s).start()

    load_first.start()
    load_second.start()

    nt = (((1,), (1,)), ((), ()))
    xp = lax.dot_general(acts_v[...], proj_v[...].reshape(pair, width), nt, preferred_element_type=f32)
    xp_own[...] = xp.astype(bf16)
    pl.semaphore_wait(barrier, len(peers))

    y_copies = [remote(xp_own, xp_in.at[j - 1], y_s.at[j - 1], y_r.at[j - 1], ydev(j)) for j in range(1, NY)]
    for j in (1, 0, 2):
        y_copies[j].start()
    row = lax.broadcasted_iota(jnp.int32, (t_count, 2 * t_count), 0)
    col = lax.broadcasted_iota(jnp.int32, (t_count, 2 * t_count), 1)
    spread = jnp.where(row == col // 2, 1.0, 0.0).astype(bf16)
    load_rows.wait()
    flat = rows_v[...].reshape(pair, rows)
    flat = jnp.concatenate([flat, flat], axis=1)
    row = lax.broadcasted_iota(jnp.int32, flat.shape, 0)
    col = lax.broadcasted_iota(jnp.int32, flat.shape, 1)
    decoder = jnp.where(row // rank == col // rows, flat.astype(f32), 0.0).T.astype(bf16)
    for copy in y_copies:
        copy.wait_recv()
    reduced = (xp + xp_in[0].astype(f32) + xp_in[1].astype(f32) + xp_in[2].astype(f32)).astype(bf16)
    weights = jnp.dot(reduced.T, spread, preferred_element_type=f32)
    row = lax.broadcasted_iota(jnp.int32, (pair, 2 * t_count), 0)
    col = lax.broadcasted_iota(jnp.int32, (pair, 2 * t_count), 1)
    weights = jnp.where(lax.rem(col, 2) == row // rank, weights, 0.0).astype(bf16)

    def core_copy(s):
        return remote(part_send.at[s, :, 1 - c], core_in.at[s], c_s.at[s], c_r.at[s], sibling)

    def x_copy(s, j):
        return remote(x_send.at[s, lax.rem(x + j, NX)], x_in.at[s, j - 1], x_s.at[s, j - 1], x_r.at[s, j - 1], xdev(j))

    def z_copy(s):
        j = offset(s)
        return remote(z_send.at[s], z_in.at[s], z_s.at[s], z_r.at[s], zdev(j))

    lag = 4

    @pl.loop(0, NZ + lag)
    def _(step):
        @pl.when(step < NZ)
        def _():
            load_group(step).wait()
            block = grads_v[step].reshape(2 * t_count, group)
            terms = jnp.dot(weights, block, preferred_element_type=f32).T.reshape(NX, NC, own, pair)
            part[step] = terms
            part_send[step] = terms.astype(bf16)
            core_copy(step).start()

        @pl.when(step >= lag)
        def _():
            s = step - lag
            core_copy(s).wait_recv()
            x_send[s] = (part[s, :, c] + core_in[s].astype(f32)).astype(bf16)
            for j in (2, 1, 3):
                x_copy(s, j).start()

    def x_sum(s):
        for j in range(1, NX):
            x_copy(s, j).wait_recv()
        total = part[s, x, c] + core_in[s, x].astype(f32)
        for j in range(NX - 1):
            total += x_in[s, j].astype(f32)
        return total

    @pl.loop(0, NZ - 1)
    def _(s):
        z_send[s] = x_sum(s).astype(bf16)
        z_copy(s).start()

    total = x_sum(NZ - 1)
    for s in range(NZ - 1):
        z_copy(s).wait_recv()
        total += z_in[s].astype(f32)
    grad = total / f32(tokens)
    load_first.wait()
    load_second.wait()
    new_first[...], new_second[...] = adam(grad, first_v[...], second_v[...])
    gathered[z, x, c] = normalize(new_first[...], new_second[...]).astype(bf16)

    def gz_copy(j):
        here = gathered.at[z, x, c]
        return remote(here, here, gz_s.at[j - 1], gz_r.at[j - 1], zdev(j))

    def gz_arrival(j):
        here = gathered.at[lax.rem(z + NZ - j, NZ), x, c]
        return remote(here, here, gz_s.at[j - 1], gz_r.at[j - 1], zdev(j))

    def near(s):
        return offset(NZ - 1 - s)

    def gx_copy(s, j):
        here = gathered.at[lax.rem(z + NZ - near(s), NZ), x, c]
        return remote(here, here, gx_s.at[s, j - 1], gx_r.at[s, j - 1], xdev(j))

    def gx_arrival(s, j):
        here = gathered.at[lax.rem(z + NZ - near(s), NZ), lax.rem(x + NX - j, NX), c]
        return remote(here, here, gx_s.at[s, j - 1], gx_r.at[s, j - 1], xdev(j))

    def gc_copy(s):
        here = gathered.at[lax.rem(z + NZ - near(s), NZ), :, c]
        return remote(here, here, gc_s.at[s], gc_r.at[s], sibling)

    def gc_arrival(s):
        here = gathered.at[lax.rem(z + NZ - near(s), NZ), :, 1 - c]
        return remote(here, here, gc_s.at[s], gc_r.at[s], sibling)

    for j in (1, 7, 2, 6, 3, 5, 4):
        gz_copy(j).start()

    x_lag, core_lag = 6, 8

    @pl.loop(0, NZ + core_lag)
    def _(step):
        @pl.when(step < NZ)
        def _():
            @pl.when(step > 0)
            def _():
                gz_arrival(near(step)).wait_recv()

            for j in (2, 1, 3):
                gx_copy(step, j).start()

        @pl.when((step >= x_lag) & (step < NZ + x_lag))
        def _():
            s = step - x_lag
            for j in range(1, NX):
                gx_arrival(s, j).wait_recv()
            gc_copy(s).start()

        @pl.when(step >= core_lag)
        def _():
            s = step - core_lag
            gc_arrival(s).wait_recv()
            g = lax.rem(z + NZ - near(s), NZ)
            block = gathered[g].reshape(group, pair)
            out = lax.dot_general(decoder, block, nt, preferred_element_type=f32)
            update[:, :, pl.ds(pl.multiple_of(g * group, 128), group)] = out.astype(bf16).reshape(2, rows, group)

    for copy in y_copies:
        copy.wait_send()
    for j in range(1, NZ):
        gz_copy(j).wait_send()

    @pl.loop(0, NZ)
    def _(s):
        core_copy(s).wait_send()
        for j in range(1, NX):
            x_copy(s, j).wait_send()

        @pl.when(s < NZ - 1)
        def _():
            z_copy(s).wait_send()

        for j in range(1, NX):
            gx_copy(s, j).wait_send()
        gc_copy(s).wait_send()


def publish(update, first, second, update_out, first_out, second_out, sem):
    pieces = update.shape[1] // 4
    copies = [
        pltpu.make_async_copy(update.at[:, pl.ds(i * pieces, pieces)], update_out.at[:, pl.ds(i * pieces, pieces)], sem.at[i])
        for i in range(4)
    ]
    copies.append(pltpu.make_async_copy(first, first_out, sem.at[4]))
    copies.append(pltpu.make_async_copy(second, second_out, sem.at[5]))
    for copy in copies:
        copy.start()
    for copy in copies:
        copy.wait()


def local(acts, out_grads, projectors, moment_first, moment_second):
    t_count, width = acts.shape
    columns = out_grads.shape[2]
    rank = projectors.shape[2]
    pair = 2 * rank
    dp_count = lax.axis_size("dp")
    own = columns // dp_count
    group = columns // NZ
    proj = jnp.swapaxes(projectors, 1, 2)
    rows = projectors.shape[1] // dp_count
    inputs = [pltpu.with_memory_space_constraint(a, pltpu.HBM) for a in (acts, proj, out_grads, moment_first, moment_second)]
    hbm = pl.BlockSpec(memory_space=pltpu.HBM)
    vmem = pl.BlockSpec(memory_space=pltpu.VMEM)
    dma = pltpu.SemaphoreType.DMA
    results = pl.pallas_call(
        functools.partial(reduce_gather, t_count * dp_count),
        out_shape=(
            pltpu.VMEM((2, rows, columns), bf16),
            pltpu.VMEM((own, pair), f32),
            pltpu.VMEM((own, pair), f32),
        ),
        in_specs=[hbm] * 5,
        out_specs=(vmem, vmem, vmem),
        scratch_shapes=[
            pltpu.VMEM((t_count, width), bf16),
            pltpu.VMEM((2, rank, width), bf16),
            pltpu.VMEM((2, rank, rows), bf16),
            pltpu.VMEM((NZ, t_count, 2, group), bf16),
            pltpu.VMEM((own, pair), f32),
            pltpu.VMEM((own, pair), f32),
            pltpu.VMEM((t_count, pair), bf16),
            pltpu.VMEM((NY - 1, t_count, pair), bf16),
            pltpu.VMEM((NZ, NX, NC, own, pair), f32),
            pltpu.VMEM((NZ, NX, NC, own, pair), bf16),
            pltpu.VMEM((NZ, NX, own, pair), bf16),
            pltpu.VMEM((NZ, NX, own, pair), bf16),
            pltpu.VMEM((NZ, NX - 1, own, pair), bf16),
            pltpu.VMEM((NZ - 1, own, pair), bf16),
            pltpu.VMEM((NZ - 1, own, pair), bf16),
            pltpu.VMEM((NZ, NX, NC, own, pair), bf16),
            dma((5,)),
            dma((NZ,)),
            dma((NY - 1,)),
            dma((NY - 1,)),
            dma((NZ,)),
            dma((NZ,)),
            dma((NZ, NX - 1)),
            dma((NZ, NX - 1)),
            dma((NZ - 1,)),
            dma((NZ - 1,)),
            dma((NZ - 1,)),
            dma((NZ - 1,)),
            dma((NZ, NX - 1)),
            dma((NZ, NX - 1)),
            dma((NZ,)),
            dma((NZ,)),
        ],
        compiler_params=pltpu.CompilerParams(collective_id=0, has_side_effects=True, vmem_limit_bytes=40 << 20),
        name="rank_adam",
    )(*inputs)
    return pl.pallas_call(
        publish,
        out_shape=tuple(jax.ShapeDtypeStruct(r.shape, r.dtype) for r in results),
        in_specs=[vmem] * 3,
        out_specs=[hbm] * 3,
        scratch_shapes=[dma((6,))],
        compiler_params=pltpu.CompilerParams(vmem_limit_bytes=4 << 20),
        name="publish",
    )(*[pltpu.with_memory_space_constraint(r, pltpu.VMEM) for r in results])


def solution(mesh):
    return jax.shard_map(
        local,
        mesh=mesh,
        in_specs=(
            P("dp", "tensor"),
            P("dp", None, "tensor"),
            P(),
            P(("tensor", "dp"), None),
            P(("tensor", "dp"), None),
        ),
        out_specs=(P(None, "dp", "tensor"), P(("tensor", "dp"), None), P(("tensor", "dp"), None)),
        check_vma=False,
    )
```

time: 65.1 us -> 49.6 us (0.76)
  Pallas kernels: 57.2 us -> 48.8 us
  local copies, waits for them, and re-layouts: 6.92 us -> 0 us
    unnamed x12 -> x0, local copies, waits for them, and re-layouts: 6.92 us -> none
    pallas_call x1, Pallas kernels: 53.2 us -> 46.9 us  [local(): pl.pallas_call(functools.partial(reduce_gather, t_count * dp_count), out_...]
    pallas_call x1, Pallas kernels: 4.02 us -> 1.9 us  [local(): pl.pallas_call(publish, out_shape=tuple((jax.ShapeDtypeStruct(r.shape, r....]
where the time goes in v2:
time: 49.6 us; the launch traced here: 49.4 us
  Pallas kernels  48.8 us (98%)
  between operations  0.64 us (1%)
    pallas_call x1, Pallas kernels, local(): pl.pallas_call(functools.partial(reduce_gather, t_count * dp_count), out_...  46.9 us
    pallas_call x1, Pallas kernels, local(): pl.pallas_call(publish, out_shape=tuple((jax.ShapeDtypeStruct(r.shape, r....  1.9 us

profile of v2, /device:TPU:1, one launch (start us, length us, event | category | flops | bytes accessed | tf_op | source)
XLA Modules:
  0.0 49.4 jit_solution(9607046202412615209)
XLA Ops:
  0.6 46.9 %rank_adam.1 = (bf16[2,128,7168]{2,1,0:T(8,128)(2,1)S(1)}, f32[112,128]{1,0:T(8,128)S(1)}, f32[112,128]{1,0:T(8,128)S(1)}) custom-call(bf16[192,2048]{1,0:T(8,128)(2,1)} %acts.1, bf16[2,64,8192]{2,1,0:T(8,128)(2,1)} %bitcast.1, bf16[192,2,7168]{2,1,0:T(2,128)(2,1)} %grads.1, f32[112,128]{1,0:T(8,128)} %first.1, f32[112,128]{1,0:T(8,128)} %second.1), custom_call_target="tpu_custom_call" | custom-call | tf_op jit(solution)/shard_map/rank_adam/pallas_call | solution.py:280
  47.5 1.9 %publish.1 = (bf16[2,128,7168]{2,1,0:T(8,128)(2,1)}, f32[112,128]{1,0:T(8,128)}, f32[112,128]{1,0:T(8,128)}) custom-call(bf16[2,128,7168]{2,1,0:T(8,128)(2,1)S(1)} %get-tuple-element.6.update, f32[112,128]{1,0:T(8,128)S(1)} %get-tuple-element.7.first, f32[112,128]{1,0:T(8,128)S(1)} %get-tuple-element.8.second), custom_call_target="tpu_custom_call" | custom-call | tf_op jit(solution)/shard_map/publish/pallas_call | solution.py:326

commit v3 on v2

--- a/solution.py
+++ b/solution.py
@@ -11,6 +11,7 @@
 corr_one = 1.0 - 0.9**10
 corr_two = 1.0 - 0.999**10
 
+HEAD = 80
 NZ, NX, NC, NY = 8, 4, 2, 4
 bf16, f32 = jnp.bfloat16, jnp.float32
 
@@ -29,9 +30,10 @@
     tokens, acts, proj, grads, first, second,
     update, new_first, new_second,
     acts_v, proj_v, rows_v, grads_v, first_v, second_v,
-    xp_own, xp_in, part, part_send, core_in, x_send, x_in, z_send, z_in, gathered,
+    xp_own, xp_in, part, part_send, core_in, x_send, x_in, z_send, z_in, tail_zin, tail_own, tail_send, tail_xin, gathered,
     in_sem, og_sem, y_s, y_r, c_s, c_r, x_s, x_r, z_s, z_r,
     gz_s, gz_r, gx_s, gx_r, gc_s, gc_r,
+    tz_s, tz_r, tx_s, tx_r, gtz_s, gtz_r, gtx_s, gtx_r,
 ):
     t_count, _, columns = grads.shape
     group = columns // NZ
@@ -51,6 +53,7 @@
     def ydev(j):
         return (dp, lax.rem(y + j, NY))
 
+    head, tail = pl.ds(0, HEAD), pl.ds(HEAD, own - HEAD)
     sibling = ((z * NX + x) * NC + (1 - c), y)
 
     def remote(src, dst, s, r, device):
@@ -120,11 +123,17 @@
         return remote(part_send.at[s, :, 1 - c], core_in.at[s], c_s.at[s], c_r.at[s], sibling)
 
     def x_copy(s, j):
-        return remote(x_send.at[s, lax.rem(x + j, NX)], x_in.at[s, j - 1], x_s.at[s, j - 1], x_r.at[s, j - 1], xdev(j))
+        return remote(x_send.at[s, lax.rem(x + j, NX), head], x_in.at[s, j - 1], x_s.at[s, j - 1], x_r.at[s, j - 1], xdev(j))
 
     def z_copy(s):
         j = offset(s)
         return remote(z_send.at[s], z_in.at[s], z_s.at[s], z_r.at[s], zdev(j))
+
+    def tz_copy(s):
+        return remote(x_send.at[s, :, tail], tail_zin.at[s], tz_s.at[s], tz_r.at[s], zdev(offset(s)))
+
+    def tx_copy(j):
+        return remote(tail_send.at[lax.rem(x + j, NX)], tail_xin.at[j - 1], tx_s.at[j - 1], tx_r.at[j - 1], xdev(j))
 
     lag = 4
 
@@ -147,47 +156,86 @@
             for j in (2, 1, 3):
                 x_copy(s, j).start()
 
+            @pl.when(s < NZ - 1)
+            def _():
+                tz_copy(s).start()
+
     def x_sum(s):
         for j in range(1, NX):
             x_copy(s, j).wait_recv()
-        total = part[s, x, c] + core_in[s, x].astype(f32)
+        total = part[s, x, c, head] + core_in[s, x, head].astype(f32)
         for j in range(NX - 1):
             total += x_in[s, j].astype(f32)
         return total
 
-    @pl.loop(0, NZ - 1)
-    def _(s):
+    def x_then_z(s):
         z_send[s] = x_sum(s).astype(bf16)
         z_copy(s).start()
 
+    pl.loop(0, 4)(x_then_z)
+    tails = part[NZ - 1, :, c, tail] + core_in[NZ - 1, :, tail].astype(f32)
+    for s in range(NZ - 1):
+        tz_copy(s).wait_recv()
+        tails += tail_zin[s].astype(f32)
+    tail_send[...] = tails.astype(bf16)
+    tail_own[...] = tails
+    for j in (2, 1, 3):
+        tx_copy(j).start()
+    pl.loop(4, NZ - 1)(x_then_z)
+
+    load_first.wait()
+    load_second.wait()
+
+    def finish(span, total):
+        grad = total / f32(tokens)
+        new_first[span], new_second[span] = adam(grad, first_v[span], second_v[span])
+        gathered[z, x, c, span] = normalize(new_first[span], new_second[span]).astype(bf16)
+
+    total = tail_own[x]
+    for j in range(1, NX):
+        tx_copy(j).wait_recv()
+        total += tail_xin[j - 1].astype(f32)
+    finish(tail, total)
     total = x_sum(NZ - 1)
     for s in range(NZ - 1):
         z_copy(s).wait_recv()
         total += z_in[s].astype(f32)
-    grad = total / f32(tokens)
-    load_first.wait()
-    load_second.wait()
-    new_first[...], new_second[...] = adam(grad, first_v[...], second_v[...])
-    gathered[z, x, c] = normalize(new_first[...], new_second[...]).astype(bf16)
+    finish(head, total)
 
     def gz_copy(j):
-        here = gathered.at[z, x, c]
+        here = gathered.at[z, x, c, head]
         return remote(here, here, gz_s.at[j - 1], gz_r.at[j - 1], zdev(j))
 
     def gz_arrival(j):
-        here = gathered.at[lax.rem(z + NZ - j, NZ), x, c]
+        here = gathered.at[lax.rem(z + NZ - j, NZ), x, c, head]
         return remote(here, here, gz_s.at[j - 1], gz_r.at[j - 1], zdev(j))
 
     def near(s):
         return offset(NZ - 1 - s)
 
     def gx_copy(s, j):
-        here = gathered.at[lax.rem(z + NZ - near(s), NZ), x, c]
+        here = gathered.at[lax.rem(z + NZ - near(s), NZ), x, c, head]
         return remote(here, here, gx_s.at[s, j - 1], gx_r.at[s, j - 1], xdev(j))
 
     def gx_arrival(s, j):
-        here = gathered.at[lax.rem(z + NZ - near(s), NZ), lax.rem(x + NX - j, NX), c]
+        here = gathered.at[lax.rem(z + NZ - near(s), NZ), lax.rem(x + NX - j, NX), c, head]
         return remote(here, here, gx_s.at[s, j - 1], gx_r.at[s, j - 1], xdev(j))
+
+    def gtx_copy(j):
+        here = gathered.at[z, x, c, tail]
+        return remote(here, here, gtx_s.at[j - 1], gtx_r.at[j - 1], xdev(j))
+
+    def gtx_arrival(j):
+        here = gathered.at[z, lax.rem(x + NX - j, NX), c, tail]
+        return remote(here, here, gtx_s.at[j - 1], gtx_r.at[j - 1], xdev(j))
+
+    def gtz_copy(j):
+        here = gathered.at[z, :, c, tail]
+        return remote(here, here, gtz_s.at[j - 1], gtz_r.at[j - 1], zdev(j))
+
+    def gtz_arrival(j):
+        here = gathered.at[lax.rem(z + NZ - j, NZ), :, c, tail]
+        return remote(here, here, gtz_s.at[j - 1], gtz_r.at[j - 1], zdev(j))
 
     def gc_copy(s):
         here = gathered.at[lax.rem(z + NZ - near(s), NZ), :, c]
@@ -197,6 +245,8 @@
         here = gathered.at[lax.rem(z + NZ - near(s), NZ), :, 1 - c]
         return remote(here, here, gc_s.at[s], gc_r.at[s], sibling)
 
+    for j in (2, 1, 3):
+        gtx_copy(j).start()
     for j in (1, 7, 2, 6, 3, 5, 4):
         gz_copy(j).start()
 
@@ -213,11 +263,23 @@
             for j in (2, 1, 3):
                 gx_copy(step, j).start()
 
+        @pl.when(step == 1)
+        def _():
+            for j in range(1, NX):
+                gtx_arrival(j).wait_recv()
+            for j in (1, 7, 2, 6, 3, 5, 4):
+                gtz_copy(j).start()
+
         @pl.when((step >= x_lag) & (step < NZ + x_lag))
         def _():
             s = step - x_lag
             for j in range(1, NX):
                 gx_arrival(s, j).wait_recv()
+
+            @pl.when(s > 0)
+            def _():
+                gtz_arrival(near(s)).wait_recv()
+
             gc_copy(s).start()
 
         @pl.when(step >= core_lag)
@@ -233,6 +295,11 @@
         copy.wait_send()
     for j in range(1, NZ):
         gz_copy(j).wait_send()
+        gtz_copy(j).wait_send()
+        tz_copy(j - 1).wait_send()
+    for j in range(1, NX):
+        tx_copy(j).wait_send()
+        gtx_copy(j).wait_send()
 
     @pl.loop(0, NZ)
     def _(s):
@@ -299,9 +366,13 @@
             pltpu.VMEM((NZ, NX, NC, own, pair), bf16),
             pltpu.VMEM((NZ, NX, own, pair), bf16),
             pltpu.VMEM((NZ, NX, own, pair), bf16),
-            pltpu.VMEM((NZ, NX - 1, own, pair), bf16),
-            pltpu.VMEM((NZ - 1, own, pair), bf16),
-            pltpu.VMEM((NZ - 1, own, pair), bf16),
+            pltpu.VMEM((NZ, NX - 1, HEAD, pair), bf16),
+            pltpu.VMEM((NZ - 1, HEAD, pair), bf16),
+            pltpu.VMEM((NZ - 1, HEAD, pair), bf16),
+            pltpu.VMEM((NZ - 1, NX, own - HEAD, pair), bf16),
+            pltpu.VMEM((NX, own - HEAD, pair), f32),
+            pltpu.VMEM((NX, own - HEAD, pair), bf16),
+            pltpu.VMEM((NX - 1, own - HEAD, pair), bf16),
             pltpu.VMEM((NZ, NX, NC, own, pair), bf16),
             dma((5,)),
             dma((NZ,)),
@@ -319,6 +390,14 @@
             dma((NZ, NX - 1)),
             dma((NZ,)),
             dma((NZ,)),
+            dma((NZ - 1,)),
+            dma((NZ - 1,)),
+            dma((NX - 1,)),
+            dma((NX - 1,)),
+            dma((NZ - 1,)),
+            dma((NZ - 1,)),
+            dma((NX - 1,)),
+            dma((NX - 1,)),
         ],
         compiler_params=pltpu.CompilerParams(collective_id=0, has_side_effects=True, vmem_limit_bytes=40 << 20),
         name="rank_adam",

time: 49.6 us -> 47.9 us (0.966)
  Pallas kernels: 48.8 us -> 47.2 us
    pallas_call x1, Pallas kernels: 46.9 us -> 45.2 us  [local(): pl.pallas_call(functools.partial(reduce_gather, t_count * dp_count), out_...]
where the time goes in v3:
time: 47.9 us; the launch traced here: 47.8 us
  Pallas kernels  47.2 us (99%)
  between operations  0.64 us (1%)
    pallas_call x1, Pallas kernels, local(): pl.pallas_call(functools.partial(reduce_gather, t_count * dp_count), out_...  45.2 us
    pallas_call x1, Pallas kernels, local(): pl.pallas_call(publish, out_shape=tuple((jax.ShapeDtypeStruct(r.shape, r....  1.9 us

profile of v3, /device:TPU:1, one launch (start us, length us, event | category | flops | bytes accessed | tf_op | source)
XLA Modules:
  0.0 47.8 jit_solution(14469248850766488562)
XLA Ops:
  0.6 45.2 %rank_adam.1 = (bf16[2,128,7168]{2,1,0:T(8,128)(2,1)S(1)}, f32[112,128]{1,0:T(8,128)S(1)}, f32[112,128]{1,0:T(8,128)S(1)}) custom-call(bf16[192,2048]{1,0:T(8,128)(2,1)} %acts.1, bf16[2,64,8192]{2,1,0:T(8,128)(2,1)} %bitcast.1, bf16[192,2,7168]{2,1,0:T(2,128)(2,1)} %grads.1, f32[112,128]{1,0:T(8,128)} %first.1, f32[112,128]{1,0:T(8,128)} %second.1), custom_call_target="tpu_custom_call" | custom-call | tf_op jit(solution)/shard_map/rank_adam/pallas_call | solution.py:347
  45.9 1.9 %publish.1 = (bf16[2,128,7168]{2,1,0:T(8,128)(2,1)}, f32[112,128]{1,0:T(8,128)}, f32[112,128]{1,0:T(8,128)}) custom-call(bf16[2,128,7168]{2,1,0:T(8,128)(2,1)S(1)} %get-tuple-element.6.update, f32[112,128]{1,0:T(8,128)S(1)} %get-tuple-element.7.first, f32[112,128]{1,0:T(8,128)S(1)} %get-tuple-element.8.second), custom_call_target="tpu_custom_call" | custom-call | tf_op jit(solution)/shard_map/publish/pallas_call | solution.py:405

commit v4 on v3

--- a/solution.py
+++ b/solution.py
@@ -12,6 +12,7 @@
 corr_two = 1.0 - 0.999**10
 
 HEAD = 80
+SLABS = 2
 NZ, NX, NC, NY = 8, 4, 2, 4
 bf16, f32 = jnp.bfloat16, jnp.float32
 
@@ -31,7 +32,7 @@
     update, new_first, new_second,
     acts_v, proj_v, rows_v, grads_v, first_v, second_v,
     xp_own, xp_in, part, part_send, core_in, x_send, x_in, z_send, z_in, tail_zin, tail_own, tail_send, tail_xin, gathered,
-    in_sem, og_sem, y_s, y_r, c_s, c_r, x_s, x_r, z_s, z_r,
+    in_sem, slab_sem, og_sem, y_s, y_r, c_s, c_r, x_s, x_r, z_s, z_r,
     gz_s, gz_r, gx_s, gx_r, gc_s, gc_r,
     tz_s, tz_r, tx_s, tx_r, gtz_s, gtz_r, gtx_s, gtx_r,
 ):
@@ -61,14 +62,23 @@
             src_ref=src, dst_ref=dst, send_sem=s, recv_sem=r, device_id=device, device_id_type=MESH
         )
 
-    load_acts = pltpu.make_async_copy(acts, acts_v, in_sem.at[0])
-    load_proj = pltpu.make_async_copy(proj.at[:, :, pl.ds(pl.multiple_of(y * width, 128), width)], proj_v, in_sem.at[1])
+    slab = width // SLABS
+
+    def load_slab(i):
+        span = pl.ds(i * slab, slab)
+        there = pl.ds(pl.multiple_of(y * width + i * slab, 128), slab)
+        return (
+            pltpu.make_async_copy(acts.at[:, span], acts_v.at[:, span], slab_sem.at[0, i]),
+            pltpu.make_async_copy(proj.at[:, :, there], proj_v.at[:, :, span], slab_sem.at[1, i]),
+        )
+
     load_first = pltpu.make_async_copy(first, first_v, in_sem.at[2])
     load_second = pltpu.make_async_copy(second, second_v, in_sem.at[3])
     rows = update.shape[1]
     load_rows = pltpu.make_async_copy(proj.at[:, :, pl.ds(pl.multiple_of(dp * rows, 128), rows)], rows_v, in_sem.at[4])
-    load_acts.start()
-    load_proj.start()
+    for i in range(SLABS):
+        for load in load_slab(i):
+            load.start()
     load_rows.start()
 
     def offset(s):
@@ -84,8 +94,16 @@
     for peer in peers:
         pl.semaphore_signal(barrier, inc=1, device_id=peer, device_id_type=MESH)
 
-    load_acts.wait()
-    load_proj.wait()
+    nt = (((1,), (1,)), ((), ()))
+    xp = None
+    for i in range(SLABS):
+        for load in load_slab(i):
+            load.wait()
+        span = pl.ds(i * slab, slab)
+        term = lax.dot_general(acts_v[:, span], proj_v[:, :, span].reshape(pair, slab), nt, preferred_element_type=f32)
+        xp = term if i == 0 else xp + term
+    xp_own[...] = xp.astype(bf16)
+    pl.semaphore_wait(barrier, len(peers))
 
     @pl.loop(0, NZ)
     def _(s):
@@ -93,11 +111,6 @@
 
     load_first.start()
     load_second.start()
-
-    nt = (((1,), (1,)), ((), ()))
-    xp = lax.dot_general(acts_v[...], proj_v[...].reshape(pair, width), nt, preferred_element_type=f32)
-    xp_own[...] = xp.astype(bf16)
-    pl.semaphore_wait(barrier, len(peers))
 
     y_copies = [remote(xp_own, xp_in.at[j - 1], y_s.at[j - 1], y_r.at[j - 1], ydev(j)) for j in range(1, NY)]
     for j in (1, 0, 2):
@@ -135,7 +148,7 @@
     def tx_copy(j):
         return remote(tail_send.at[lax.rem(x + j, NX)], tail_xin.at[j - 1], tx_s.at[j - 1], tx_r.at[j - 1], xdev(j))
 
-    lag = 4
+    lag = 3
 
     @pl.loop(0, NZ + lag)
     def _(step):
@@ -144,9 +157,9 @@
             load_group(step).wait()
             block = grads_v[step].reshape(2 * t_count, group)
             terms = jnp.dot(weights, block, preferred_element_type=f32).T.reshape(NX, NC, own, pair)
-            part[step] = terms
             part_send[step] = terms.astype(bf16)
             core_copy(step).start()
+            part[step] = terms
 
         @pl.when(step >= lag)
         def _():
@@ -250,7 +263,7 @@
     for j in (1, 7, 2, 6, 3, 5, 4):
         gz_copy(j).start()
 
-    x_lag, core_lag = 6, 8
+    x_lag, core_lag = 7, 10
 
     @pl.loop(0, NZ + core_lag)
     def _(step):
@@ -262,6 +275,15 @@
 
             for j in (2, 1, 3):
                 gx_copy(step, j).start()
+
+            core_copy(step).wait_send()
+            for j in range(1, NX):
+                x_copy(step, j).wait_send()
+
+            @pl.when(step < NZ - 1)
+            def _():
+                z_copy(step).wait_send()
+                tz_copy(step).wait_send()
 
         @pl.when(step == 1)
         def _():
@@ -269,6 +291,10 @@
                 gtx_arrival(j).wait_recv()
             for j in (1, 7, 2, 6, 3, 5, 4):
                 gtz_copy(j).start()
+            for j in range(1, NX):
+                y_copies[j - 1].wait_send()
+                tx_copy(j).wait_send()
+                gtx_copy(j).wait_send()
 
         @pl.when((step >= x_lag) & (step < NZ + x_lag))
         def _():
@@ -290,30 +316,13 @@
             block = gathered[g].reshape(group, pair)
             out = lax.dot_general(decoder, block, nt, preferred_element_type=f32)
             update[:, :, pl.ds(pl.multiple_of(g * group, 128), group)] = out.astype(bf16).reshape(2, rows, group)
-
-    for copy in y_copies:
-        copy.wait_send()
+            gc_copy(s).wait_send()
+            for j in range(1, NX):
+                gx_copy(s, j).wait_send()
+
     for j in range(1, NZ):
         gz_copy(j).wait_send()
         gtz_copy(j).wait_send()
-        tz_copy(j - 1).wait_send()
-    for j in range(1, NX):
-        tx_copy(j).wait_send()
-        gtx_copy(j).wait_send()
-
-    @pl.loop(0, NZ)
-    def _(s):
-        core_copy(s).wait_send()
-        for j in range(1, NX):
-            x_copy(s, j).wait_send()
-
-        @pl.when(s < NZ - 1)
-        def _():
-            z_copy(s).wait_send()
-
-        for j in range(1, NX):
-            gx_copy(s, j).wait_send()
-        gc_copy(s).wait_send()
 
 
 def publish(update, first, second, update_out, first_out, second_out, sem):
@@ -375,6 +384,7 @@
             pltpu.VMEM((NX - 1, own - HEAD, pair), bf16),
             pltpu.VMEM((NZ, NX, NC, own, pair), bf16),
             dma((5,)),
+            dma((2, SLABS)),
             dma((NZ,)),
             dma((NY - 1,)),
             dma((NY - 1,)),

time: 47.9 us -> 47.6 us (level)
  no operation moved by 1% of the time
where the time goes in v4:
time: 47.6 us; the launch traced here: 47.5 us
  Pallas kernels  46.9 us (99%)
  between operations  0.64 us (1%)
    pallas_call x1, Pallas kernels, local(): pl.pallas_call(functools.partial(reduce_gather, t_count * dp_count), out_...  45 us
    pallas_call x1, Pallas kernels, local(): pl.pallas_call(publish, out_shape=tuple((jax.ShapeDtypeStruct(r.shape, r....  1.9 us

profile of v4, /device:TPU:1, one launch (start us, length us, event | category | flops | bytes accessed | tf_op | source)
XLA Modules:
  0.0 47.5 jit_solution(10161746738110410007)
XLA Ops:
  0.6 45.0 %rank_adam.1 = (bf16[2,128,7168]{2,1,0:T(8,128)(2,1)S(1)}, f32[112,128]{1,0:T(8,128)S(1)}, f32[112,128]{1,0:T(8,128)S(1)}) custom-call(bf16[192,2048]{1,0:T(8,128)(2,1)} %acts.1, bf16[2,64,8192]{2,1,0:T(8,128)(2,1)} %bitcast.1, bf16[192,2,7168]{2,1,0:T(2,128)(2,1)} %grads.1, f32[112,128]{1,0:T(8,128)} %first.1, f32[112,128]{1,0:T(8,128)} %second.1), custom_call_target="tpu_custom_call" | custom-call | tf_op jit(solution)/shard_map/rank_adam/pallas_call | solution.py:356
  45.6 1.9 %publish.1 = (bf16[2,128,7168]{2,1,0:T(8,128)(2,1)}, f32[112,128]{1,0:T(8,128)}, f32[112,128]{1,0:T(8,128)}) custom-call(bf16[2,128,7168]{2,1,0:T(8,128)(2,1)S(1)} %get-tuple-element.6.update, f32[112,128]{1,0:T(8,128)S(1)} %get-tuple-element.7.first, f32[112,128]{1,0:T(8,128)S(1)} %get-tuple-element.8.second), custom_call_target="tpu_custom_call" | custom-call | tf_op jit(solution)/shard_map/publish/pallas_call | solution.py:415

commit v5 on v4

--- a/solution.py
+++ b/solution.py
@@ -289,7 +289,7 @@
         def _():
             for j in range(1, NX):
                 gtx_arrival(j).wait_recv()
-            for j in (1, 7, 2, 6, 3, 5, 4):
+            for j in (4, 3, 5, 2, 6, 1, 7):
                 gtz_copy(j).start()
             for j in range(1, NX):
                 y_copies[j - 1].wait_send()

time: 47.6 us -> 49.2 us (1.034)
  Pallas kernels: 46.9 us -> 48.4 us
    pallas_call x1, Pallas kernels: 45 us -> 46.5 us  [local(): pl.pallas_call(functools.partial(reduce_gather, t_count * dp_count), out_...]
where the time goes in v5:
time: 49.2 us; the launch traced here: 49.1 us
  Pallas kernels  48.4 us (98%)
  between operations  0.64 us (1%)
    pallas_call x1, Pallas kernels, local(): pl.pallas_call(functools.partial(reduce_gather, t_count * dp_count), out_...  46.5 us
    pallas_call x1, Pallas kernels, local(): pl.pallas_call(publish, out_shape=tuple((jax.ShapeDtypeStruct(r.shape, r....  1.9 us

profile of v5, /device:TPU:1, one launch (start us, length us, event | category | flops | bytes accessed | tf_op | source)
XLA Modules:
  0.0 49.1 jit_solution(3809556453513002468)
XLA Ops:
  0.6 46.5 %rank_adam.1 = (bf16[2,128,7168]{2,1,0:T(8,128)(2,1)S(1)}, f32[112,128]{1,0:T(8,128)S(1)}, f32[112,128]{1,0:T(8,128)S(1)}) custom-call(bf16[192,2048]{1,0:T(8,128)(2,1)} %acts.1, bf16[2,64,8192]{2,1,0:T(8,128)(2,1)} %bitcast.1, bf16[192,2,7168]{2,1,0:T(2,128)(2,1)} %grads.1, f32[112,128]{1,0:T(8,128)} %first.1, f32[112,128]{1,0:T(8,128)} %second.1), custom_call_target="tpu_custom_call" | custom-call | tf_op jit(solution)/shard_map/rank_adam/pallas_call | solution.py:356
  47.2 1.9 %publish.1 = (bf16[2,128,7168]{2,1,0:T(8,128)(2,1)}, f32[112,128]{1,0:T(8,128)}, f32[112,128]{1,0:T(8,128)}) custom-call(bf16[2,128,7168]{2,1,0:T(8,128)(2,1)S(1)} %get-tuple-element.6.update, f32[112,128]{1,0:T(8,128)S(1)} %get-tuple-element.7.first, f32[112,128]{1,0:T(8,128)S(1)} %get-tuple-element.8.second), custom_call_target="tpu_custom_call" | custom-call | tf_op jit(solution)/shard_map/publish/pallas_call | solution.py:415
